TPU v7x, 32 devices: a whole 2x2x4 slice. The times are simulated.
32 devices in a mesh: dp: 8 (over z, y), head: 4 (over x, core).
Axes of the slice: x: 2, y: 2, z: 4, core: 2. Of those that a mesh axis runs over, the one named last changes fastest.
Arguments:
- images: bfloat16 [16, 32, 32, 384], P('dp', 'head'), may hold values from -16 to 16
- noise_field: bfloat16 [16, 32, 32, 384], P('dp', 'head'), may hold values from -6 to 6
- time_steps: int32 [16], P('dp'), may hold values from 0 to 3999
- embedding: bfloat16 [16, 768], P('dp'), may hold values from -5 to 5
- first_kernel: bfloat16 [3, 3, 384, 384], P(None, None, 'dp', 'head'), may hold values from -0.109375 to 0.109375
- second_kernel: bfloat16 [3, 3, 384, 384], P(None, None, 'dp', 'head'), may hold values from -0.109375 to 0.109375
- film_weight: bfloat16 [768, 768], P('dp', 'head'), may hold values from -0.21875 to 0.21875
- attend_weight: bfloat16 [384, 1152], P('dp', 'head'), may hold values from -0.3125 to 0.3125
- output_weight: bfloat16 [384, 384], P('dp', 'head'), may hold values from -1.25 to 1.25
- norm_gains: float32 [3, 384], replicated, may hold values from 0.1 to 1.9
- biases: float32 [10, 384], replicated, may hold values from -3 to 3
- cotangent: bfloat16 [16, 32, 32, 384], P('dp', 'head'), may hold values from -6 to 6
Outputs:
- result: float32 [16, 32, 32, 384], P('dp', 'head')
- image_grad: float32 [16, 32, 32, 384], P('dp', 'head')
- embed_grad: float32 [16, 768], P('dp')
- first_grad: float32 [3, 3, 384, 384], P(None, None, 'dp', 'head')
- second_grad: float32 [3, 3, 384, 384], P(None, None, 'dp', 'head')
- film_grad: float32 [768, 768], P('dp', 'head')
- attend_grad: float32 [384, 1152], P('dp', 'head')
- output_grad: float32 [384, 384], P('dp', 'head')
- gains_grad: float32 [3, 384], replicated
- biases_grad: float32 [10, 384], replicated
All inputs are finite; a program needn't handle non-finite values.
Results may differ from a plain program's by a relative error of at most 0.015.
Values may be sent and summed in bfloat16 or wider, within the bound.
A program may use at most 128 MiB of HBM per device.

v0:
```python
import math

import jax
import jax.numpy as jnp
import numpy as np
from jax import lax
from jax.experimental import pallas as pl
from jax.experimental.pallas import tpu as pltpu
from jax.sharding import PartitionSpec as P

HEAD_DIM = 96
GROUPS = 32
STEPS = 4000
EPS = 1e-05
OFFSET = 0.008
MESH = pl.DeviceIdType.MESH
F32 = jnp.float32
BF16 = jnp.bfloat16

PX = 1024
ROW = 32
CHUNK = 256
BLK = 96
HALF = 256
NHEAD = 4


def plan(time_step, lanes):
    fraction = (jnp.full((1, lanes), time_step, jnp.int32).astype(F32) + 1.0) / STEPS
    start = math.cos(OFFSET / (1.0 + OFFSET) * (math.pi / 2)) ** 2
    curve = jnp.square(jnp.cos((fraction + OFFSET) / (1.0 + OFFSET) * (math.pi / 2))) / start
    return (jnp.sqrt(curve), jnp.sqrt(jnp.maximum(1.0 - curve, 0.0)))


def channel_lanes():
    sel = np.zeros((2, 384, HALF), np.float32)
    for block in range(4):
        for j in range(BLK):
            sel[block % 2, block * BLK + j, (block // 2) * 128 + j] = 1.0
    return sel


def block_lanes(count):
    sel = np.zeros((count * BLK, count * 128), np.float32)
    for block in range(count):
        for j in range(BLK):
            sel[block * BLK + j, block * 128 + j] = 1.0
    return sel


def group_mask():
    lane = np.arange(HALF)
    ok = lane % 128 < BLK
    group = (lane // 128) * 100 + (lane % 128) // 12
    return ((group[:, None] == group[None, :]) & ok[:, None] & ok[None, :]).astype(np.float32)


def dot(a, b):
    return lax.dot_general(a, b, (((1,), (0,)), ((), ())), preferred_element_type=F32)


def dot_nt(a, b):
    return lax.dot_general(a, b, (((1,), (1,)), ((), ())), preferred_element_type=F32)


def dot_nt_high(a, b):
    return lax.dot_general(
        a, b, (((1,), (1,)), ((), ())), preferred_element_type=F32, precision=lax.Precision.HIGHEST
    )


def dot_tn_high(a, b):
    return lax.dot_general(
        a, b, (((0,), (0,)), ((), ())), preferred_element_type=F32, precision=lax.Precision.HIGHEST
    )


def exact_dot(values, ones):
    high = values.astype(BF16).astype(F32)
    rest = values - high
    middle = rest.astype(BF16).astype(F32)
    low = rest - middle
    rows = values.shape[0]
    out = dot(jnp.concatenate([high, middle, low], axis=0).astype(BF16), ones)
    return out[:rows] + out[rows : 2 * rows] + out[2 * rows :]


def sigmoid(v):
    return 0.5 + 0.5 * jnp.tanh(0.5 * v)


def silu(v):
    return v * sigmoid(v)


def silu_slope(v):
    s = sigmoid(v)
    return s * (1.0 + v * (1.0 - s))


def pack_taps(t0, t1, t2):
    t0, t1, t2 = t0[:, :BLK], t1[:, :BLK], t2[:, :BLK]
    join = lambda a, b: jnp.concatenate([a, b], axis=1)
    return jnp.concatenate(
        [
            join(t0[:32], t2[:32, :32]),
            join(t0[32:], t2[:16, 32:64]),
            join(t1[:16], t2[16:32, 32:64]),
            join(t1[16:], t2[:32, 64:]),
            join(t2[32:], jnp.zeros((16, 32), t2.dtype)),
        ],
        axis=0,
    )


def last_tap(packed):
    lanes = [packed[:32, BLK:], packed[32:64, BLK:], packed[64:96, BLK:], jnp.zeros((32, 32), packed.dtype)]
    return jnp.concatenate([jnp.concatenate(lanes, axis=1), packed[96:112]], axis=0)


def pack_four(b0, b1, b2, b3):
    return jnp.concatenate(
        [jnp.concatenate([b[:, :BLK], b3[:, 32 * k : 32 * k + 32]], axis=1) for k, b in enumerate((b0, b1, b2))],
        axis=0,
    )


def unpack_four(packed):
    size = packed.shape[0] // 3
    parts = [packed[k * size : k * size + size] for k in range(3)]
    zero = jnp.zeros((size, 32), packed.dtype)
    fourth = jnp.concatenate([p[:, BLK:] for p in parts] + [zero], axis=1)
    return [jnp.concatenate([p[:, :BLK], zero], axis=1) for p in parts] + [fourth]


def pack_pixels(full):
    half = CHUNK // 2
    return pack_four(full[:half, :128], full[half:, :128], full[:half, 128:], full[half:, 128:])


def unpack_pixels(packed):
    b0, b1, b2, b3 = unpack_four(packed)
    return jnp.concatenate([jnp.concatenate([b0, b2], axis=1), jnp.concatenate([b1, b3], axis=1)], axis=0)


INPUTS = (
    "steps",
    "images",
    "noise",
    "cot",
    "emb",
    "k1",
    "k2",
    "wf",
    "wa",
    "wo",
    "gains",
    "biases",
    "sel",
    "gmask",
    "selp",
)
OUTPUTS = (
    "ro_dst",
    "io_dst",
    "embed_grad",
    "first",
    "second",
    "film",
    "attend",
    "output",
    "gains_out",
    "biases_out",
)


FAR = (
    "images",
    "noise",
    "cot",
    "sel",
    "selp",
    "k2",
    "wa",
    "wf",
    "gmask",
)


class Names:
    def __init__(self, names, refs):
        for name, ref in zip(names, refs):
            setattr(self, name, ref)


def scratch_list(n, inside, inputs):
    dma = pltpu.SemaphoreType.DMA
    items = []

    def vm(name, shape, dtype):
        items.append((name, pltpu.VMEM(shape, dtype)))

    def sem(name, count):
        items.append((name + "_s", dma((count,))))
        items.append((name + "_r", dma((count,))))

    for name in FAR:
        vm(name, inputs[name].shape, inputs[name].dtype)
    items.append(("far_s", dma((len(FAR),))))
    for name in ("mx", "cx", "ro", "io"):
        vm(name + "_src", (4, 384, 128), BF16)
        if name in ("mx", "cx"):
            vm(name + "_dst", (4, 384, 128), BF16)
            vm(name, (4, CHUNK, HALF), BF16)
        sem(name, 4)
    for name in ("act1", "act2"):
        vm(name, (2, PX + 2 * ROW, HALF), BF16)
        vm(name + "_t", (2, HALF, PX), BF16)
        sem(name, 4)
        sem(name + "_t", 1)
    vm("ai", (2, PX, HALF), BF16)
    vm("ai_t", (2, HALF, PX), BF16)
    sem("ai_t", 1)
    sem("ai", 4)
    vm("att", (4, PX, 128), BF16)
    vm("att_t", (2, HALF, PX), BF16)
    sem("att", 4)
    for name in ("do", "n3", "d2", "d1"):
        vm(name + "_src", (PX, HALF), BF16)
        vm(name + "_dst", (PX, HALF), BF16)
        sem(name, 2)
    vm("v2", (PX, HALF), F32)
    vm("v3", (PX, HALF), F32)
    vm("gres", (PX, HALF), F32)
    vm("gtmp", (PX, HALF), F32)
    vm("qkv", (6, PX, 128), BF16)
    vm("kvt", (4, 128, PX), BF16)
    vm("dout", (2, PX, 128), BF16)
    vm("dproj", (6, PX, 128), BF16)
    vm("gr2", (3, PX + 2 * ROW, HALF), BF16)
    vm("gr1", (3, PX + 2 * ROW, HALF), BF16)
    vm("par", (16, 384), F32)
    vm("parown", (16, HALF), F32)
    vm("stat", (16, HALF), F32)
    vm("sums", (16, HALF), F32)
    if inside:
        vm("g1", (4, 4, 336, 128), BF16)
        vm("g2", (4, 4, 336, 128), BF16)
        vm("t1", (4, 4, 144, 128), BF16)
        vm("t2", (4, 4, 144, 128), BF16)
        vm("p3", (4, 4, 144, 128), BF16)
        vm("g3", (4, 4, 192, 128), BF16)
        for name in ("g1", "g2", "p3"):
            sem(name + "z", 4)
            sem(name + "v", 4)
            sem(name + "w", 8)
        vm("sw_src", (48, 128), BF16)
        vm("sw_dst", (48, 128), BF16)
        sem("sw", 1)
        vm("sb_src", (48, 128), F32)
        vm("sb_dst", (48, 128), F32)
        sem("sb", 1)
        for name, nc, rows in (("r1", 3, 112), ("r2", 3, 112), ("r3", 1, 144)):
            vm(name + "_acc", (nc, 4, 4, rows, 128), BF16)
            vm(name + "_own", (nc, rows, 128), F32)
            vm(name + "w_dst", (nc, 2, 4, rows, 128), BF16)
            vm(name + "v_src", (nc, 4, rows, 128), BF16)
            vm(name + "v_dst", (nc, 4, rows, 128), BF16)
            vm(name + "z_src", (4, nc, rows, 128), BF16)
            vm(name + "z_dst", (4, nc, rows, 128), BF16)
            sem(name + "w", nc)
            sem(name + "v", nc)
            sem(name + "z", nc * 4)
    vm("el", (n, 2, 768), F32)
    sem("el", n)
    vm("em", (2 * n, 768), F32)
    vm("wfp", (128, HALF), BF16)
    vm("esel", (2 * n, 128), F32)
    vm("fp", (n, 2, HALF), F32)
    vm("fr", (n, 2, HALF), F32)
    sem("fr", n)
    vm("fx", (4, 1, 128), F32)
    vm("fh", (4, 1, 128), F32)
    sem("fh", 4)
    vm("ft", (4, 1, 128), F32)
    vm("th", (4, 1, 128), F32)
    sem("th", 4)
    vm("fa", (n, 2, HALF), F32)
    sem("fa", n)
    vm("fta", (2 * n, HALF), F32)
    vm("ep", (n, 2, 128), F32)
    vm("er", (n, 2, 128), F32)
    sem("er", n)
    vm("eh", (4, n, 2, 128), F32)
    sem("eh", 4)
    vm("ad", (n, 16, HALF), F32)
    sem("ad", n)
    vm("hb", (4, 16, HALF), F32)
    sem("hb", 4)
    return items


def make_kernel(n, inside, names):
    film_rows = 768 // n

    def kernel(*refs):
        r = Names(names, refs)
        d = lax.axis_index("dp")
        h = lax.axis_index("head")
        x = h // 2
        c = h - 2 * x
        z = d // 2
        y = d - 2 * z
        sib = (d, h + 1 - 2 * c)
        xdev = (d, h + 2 - 4 * x)
        v = x + c * (y - x)
        w = y + c * (x - y)
        vdev = (d + c * (1 - 2 * y), h + (1 - c) * (2 - 4 * x))
        wdev = (d + (1 - c) * (1 - 2 * y), h + c * (2 - 4 * x))

        def slot(xx, yy, o=c):
            if inside:
                return (yy + o * (xx - yy)) * 2 + xx + o * (yy - xx)
            return yy * 2 + xx

        def order(split, i):
            return c * (i // 2) if split else c

        def rc(src, dst, send, recv, dev):
            return pltpu.make_async_remote_copy(
                src_ref=src, dst_ref=dst, send_sem=send, recv_sem=recv, device_id=dev, device_id_type=MESH
            )

        def loop(count, body):
            def step(i, carry):
                body(i)
                return carry

            lax.fori_loop(0, count, step, 0)

        def each(count, body):
            for i in range(count):
                body(i)

        def rows(i, size=CHUNK, base=0):
            return pl.ds(pl.multiple_of(base + i * size, 32), size)

        def dp_start(src_of, dst, send, recv):
            def step(k, carry):
                peer = lax.rem(d + k, n)
                rc(src_of(peer), dst.at[d], send.at[k], recv.at[d], (peer, h)).start()
                return carry

            lax.fori_loop(1, n, step, 0)

        def dp_wait(src_of, dst, send, recv):
            def step(k, carry):
                peer = lax.rem(d + k, n)
                copy = rc(src_of(peer), dst.at[peer], send.at[k], recv.at[peer], (peer, h))
                copy.wait_recv()
                copy.wait_send()
                return carry

            lax.fori_loop(1, n, step, 0)

        def head_start(src_of, dst, send, recv):
            for k in range(1, 4):
                peer = lax.rem(h + k, 4)
                rc(src_of(peer), dst.at[h], send.at[k], recv.at[h], (d, peer)).start()

        def head_wait(src_of, dst, send, recv):
            for k in range(1, 4):
                peer = lax.rem(h + k, 4)
                copy = rc(src_of(peer), dst.at[peer], send.at[k], recv.at[peer], (d, peer))
                copy.wait_recv()
                copy.wait_send()

        class Halves:
            def __init__(self, name, base):
                self.buf, self.base = getattr(r, name), base
                self.send, self.recv = getattr(r, name + "_s"), getattr(r, name + "_r")

            def at(self, core, i):
                return self.buf.at[core, rows(i, CHUNK, self.base)]

            def fill(self, make):
                def body(i):
                    self.buf[c, rows(i, CHUNK, self.base), :] = make(i)
                    ref = self.at(c, i)
                    rc(ref, ref, self.send.at[i], self.recv.at[i], sib).start()

                loop(4, body)

            def wait(self):
                for i in range(4):
                    ref = self.at(1 - c, i)
                    copy = rc(ref, ref, self.send.at[i], self.recv.at[i], sib)
                    copy.wait_recv()
                    copy.wait_send()

        class Parts:
            def __init__(self, name):
                self.src, self.dst = getattr(r, name + "_src"), getattr(r, name + "_dst")
                self.send, self.recv = getattr(r, name + "_s"), getattr(r, name + "_r")

            def copy(self, i):
                at = rows(i, 2 * CHUNK)
                return rc(self.src.at[at], self.dst.at[at], self.send.at[i], self.recv.at[i], sib)

            def fill(self, make):
                def body(i):
                    self.src[rows(i, 2 * CHUNK), :] = make(i).astype(BF16)
                    self.copy(i).start()

                each(2, body)

            def get(self, i):
                copy = self.copy(i)
                copy.wait_recv()
                copy.wait_send()
                return self.dst[rows(i, 2 * CHUNK), :].astype(F32)

        class Gather:
            def __init__(self, name, split):
                self.g, self.split = getattr(r, name), split
                self.zs, self.zr = getattr(r, name + "z_s"), getattr(r, name + "z_r")
                self.vs, self.vr = getattr(r, name + "v_s"), getattr(r, name + "v_r")
                self.ws, self.wr = getattr(r, name + "w_s"), getattr(r, name + "w_r")

            def at(self, i, far_w, far_v):
                o = order(self.split, i)
                vv, ww = x + o * (y - x), y + o * (x - y)
                return (ww + far_w * (1 - 2 * ww)) * 2 + vv + far_v * (1 - 2 * vv)

            def zcopy(self, k):
                peer = (lax.rem(z + k, 4) * 2 + y, h)
                src, dst = self.g.at[self.at(0, 0, 0), 0], self.g.at[self.at(4 - k, 0, 0), 4 - k]
                return rc(src, dst, self.zs.at[k], self.zr.at[4 - k], peer)

            def vcopy(self, far_v, i):
                o = order(self.split, i)
                ref = self.g.at[self.at(i, 0, far_v), i]
                dev = (d + o * (1 - 2 * y), h + (1 - o) * (2 - 4 * x))
                return rc(ref, ref, self.vs.at[i], self.vr.at[i], dev)

            def wcopy(self, far_w, far_v, i):
                o = order(self.split, i)
                ref = self.g.at[self.at(i, far_w, far_v), i]
                dev = (d + (1 - o) * (1 - 2 * y), h + o * (2 - 4 * x))
                return rc(ref, ref, self.ws.at[2 * i + far_v], self.wr.at[2 * i + far_v], dev)

            def own(self):
                for k in range(1, 4):
                    self.zcopy(k).start()
                self.vcopy(0, 0).start()
                self.wcopy(0, 0, 0).start()

            def pass_own(self):
                self.vcopy(1, 0).wait_recv()
                self.wcopy(0, 1, 0).start()

            def pass_z(self, *ks):
                for k in ks:
                    self.zcopy(k).wait_recv()
                    self.vcopy(0, 4 - k).start()
                    self.wcopy(0, 0, 4 - k).start()

            def pass_v(self, *ks):
                for k in ks:
                    self.vcopy(1, 4 - k).wait_recv()
                    self.wcopy(0, 1, 4 - k).start()

            def take(self, blocks):
                for i, far_v in ((0, 0), (0, 1), (3, 0), (1, 0), (2, 0), (3, 1), (1, 1), (2, 1)):
                    self.wcopy(1, far_v, i).wait_recv()
                    blocks.unpack([(self.at(i, 1, far_v), i)])

            def finish(self):
                for k in range(1, 4):
                    self.zcopy(k).wait_send()
                for i in range(4):
                    self.vcopy(0, i).wait_send()
                    for far_v in range(2):
                        self.wcopy(0, far_v, i).wait_send()

            def blocks(self, far_w):
                return [(self.at(i, far_w, far_v), i) for i in range(4) for far_v in range(2)]

        class Reduce:
            def __init__(self, name, count):
                get = lambda tail: getattr(r, name + tail)
                self.acc, self.count = get("_acc"), count
                self.wdst, self.ws, self.wr, self.own = get("w_dst"), get("w_s"), get("w_r"), get("_own")
                self.vsrc, self.vdst, self.vs, self.vr = get("v_src"), get("v_dst"), get("v_s"), get("v_r")
                self.zsrc, self.zdst, self.zs, self.zr = get("z_src"), get("z_dst"), get("z_s"), get("z_r")

            def wcopy(self, a):
                ref = self.acc.at[a, pl.ds((1 - w) * 2, 2)]
                return rc(ref, self.wdst.at[a], self.ws.at[a], self.wr.at[a], wdev)

            def vcopy(self, a, size):
                at = pl.ds(a, size)
                return rc(self.vsrc.at[at], self.vdst.at[at], self.vs.at[a], self.vr.at[a], vdev)

            def zcopy(self, a, size, k):
                at = pl.ds(a, size)
                return rc(
                    self.zsrc.at[k, at],
                    self.zdst.at[4 - k, at],
                    self.zs.at[a * 4 + k],
                    self.zr.at[a * 4 + 4 - k],
                    (lax.rem(z + k, 4) * 2 + y, h),
                )

            def start(self, a):
                self.wcopy(a).start()

            def second(self, first, size):
                for a in range(first, first + size):
                    self.wcopy(a).wait_recv()

                    def step(zz, carry):
                        self.vsrc[a, zz] = (
                            self.acc[a, w * 2 + 1 - v, zz].astype(F32) + self.wdst[a, 1 - v, zz].astype(F32)
                        ).astype(BF16)
                        return carry

                    lax.fori_loop(0, 4, step, 0)
                self.vcopy(first, size).start()

            def third(self, first, size):
                self.vcopy(first, size).wait_recv()
                for a in range(first, first + size):

                    for k in range(4):
                        zz = lax.rem(z + k, 4)
                        total = (
                            self.acc[a, w * 2 + v, zz].astype(F32)
                            + self.wdst[a, v, zz].astype(F32)
                            + self.vdst[a, zz].astype(F32)
                        )
                        if k == 0:
                            self.own[a] = total
                        else:
                            self.zsrc[k, a] = total.astype(BF16)
                for k in range(1, 4):
                    self.zcopy(first, size, k).start()

            def finish(self, groups):
                for first, size in groups:
                    self.vcopy(first, size).wait_send()
                    for k in range(1, 4):
                        copy = self.zcopy(first, size, k)
                        copy.wait_recv()
                        copy.wait_send()
                for a in range(self.count):
                    self.wcopy(a).wait_send()

            def last(self, a):
                total = self.own[a]
                for k in range(1, 4):
                    total = total + self.zdst[k, a].astype(F32)
                return total

        def rel(zc):
            return lax.rem(zc - z + 4, 4) if inside else zc

        def where_is(split, xx, yy, zc):
            i = rel(zc)
            return slot(xx, yy, order(split, i)), i

        class Taps:
            def __init__(self, packed, last, split):
                self.packed, self.last, self.split = packed, last, split

            def block(self, tap, zc, xx, yy):
                a, b = tap // 3, tap % 3
                q, i = where_is(self.split, xx, yy, zc)
                if b < 2:
                    return self.packed[q, i, pl.ds(a * 112 + b * 48, 48), :]
                return self.last[q, i, pl.ds(a * 48, 48), :]

            def unpack(self, places):
                for q, i in places:
                    for a in range(3):
                        self.last[q, i, pl.ds(a * 48, 48), :] = last_tap(self.packed[q, i, pl.ds(a * 112, 112), :])

        class Plain:
            def __init__(self, blocks, split):
                self.blocks, self.split = blocks, split

            def block(self, tap, zc, xx, yy):
                q, i = where_is(self.split, xx, yy, zc)
                return self.blocks[q, i, pl.ds(tap * 48, 48), :]

            def unpack(self, places):
                for q, i in places:
                    self.blocks[q, i] = jnp.concatenate(unpack_four(r.p3[q, i]), axis=0)

        k1, k2, k3 = Taps(r.g1, r.t1, True), Taps(r.g2, r.t2, False), Plain(r.g3, True)

        def wtile(g, tap, zc, xx):
            return jnp.concatenate(
                [g.block(tap, zc, xx, 0), g.block(tap, zc, xx, 1), jnp.zeros((32, 128), BF16)], axis=0
            )

        def wtap(g, tap, zcs):
            return jnp.concatenate(
                [jnp.concatenate([wtile(g, tap, zc, xx) for xx in range(2)], axis=1) for zc in zcs], axis=0
            )

        ALL = (0, 2, 1, 3)

        def half_of(core):
            return (core, core + 2)

        def wproj(zcs):
            return jnp.concatenate(
                [
                    jnp.concatenate([wtile(k3, j, zc, xx) for xx in range(2) for j in range(3)], axis=1)
                    for zc in zcs
                ],
                axis=0,
            )

        def flat(buf, base, i, size):
            return jnp.concatenate([buf[0, rows(i, size, base), :], buf[1, rows(i, size, base), :]], axis=1)

        barrier = pltpu.get_barrier_semaphore()

        def greet(k, carry):
            pl.semaphore_signal(barrier, inc=1, device_id=(lax.rem(d + k, n), h), device_id_type=MESH)
            return carry

        lax.fori_loop(1, n, greet, 0)
        for k in range(1, 4):
            pl.semaphore_signal(barrier, inc=1, device_id=(d, lax.rem(h + k, 4)), device_id_type=MESH)
        def fetch(name):
            return pltpu.make_async_copy(getattr(r, name + "_far"), getattr(r, name), r.far_s.at[FAR.index(name)])

        for name in FAR:
            fetch(name).start()
        if inside:
            ga, gb, gc = Gather("g1", True), Gather("g2", False), Gather("p3", True)
            for a in range(3):
                r.g1[ga.at(0, 0, 0), 0, pl.ds(a * 112, 112), :] = pack_taps(*[r.k1[3 * a + b] for b in range(3)])
        pl.semaphore_wait(barrier, n - 1 + 3)
        if inside:
            ga.own()

        for name in FAR:
            fetch(name).wait()
        def head_copy(src, dst, send, recv, k):
            peer = lax.rem(h + k, 4)
            return rc(src.at[peer], dst.at[h], send.at[k], recv.at[h], (d, peer))

        for step in range(2):
            m = x + (1 - step) * (1 - 2 * x)
            keep, spread = plan(r.steps[m], 384)
            low = (keep * r.images[m].astype(F32) + spread * r.noise[m].astype(F32)).astype(BF16)
            for core in range(2):
                r.mx_src[m * 2 + core] = pack_pixels(dot(low, r.sel[core])).astype(BF16)
            for k in (2, 3 - 2 * c) if step == 0 else (1 + 2 * c,):
                head_copy(r.mx_src, r.mx_dst, r.mx_s, r.mx_r, k).start()
        r.mx_dst[h] = r.mx_src[h]
        if inside:
            ga.pass_own()

        r.el[d] = silu(r.emb[...].astype(F32)).astype(BF16).astype(F32)
        dp_start(lambda p: r.el.at[d], r.el, r.el_s, r.el_r)

        if inside:
            blocks = dot(r.wa[...], r.selp[: 3 * BLK, : 3 * 128]).astype(BF16)
            r.sw_src[...] = blocks[:, 128:256]
            swap = rc(r.sw_src, r.sw_dst, r.sw_s.at[0], r.sw_r.at[0], sib)
            swap.start()
            for a in range(3):
                r.g2[gb.at(0, 0, 0), 0, pl.ds(a * 112, 112), :] = pack_taps(*[r.k2[3 * a + b] for b in range(3)])
        r.par[0:3, :] = r.gains[...]
        r.par[3:13, :] = r.biases[...]
        r.par[13:16, :] = jnp.zeros((3, 384), F32)
        r.parown[...] = exact_dot(r.par[...], r.sel[c])

        def prow(i):
            return r.parown[pl.ds(i, 1), :]

        for buf in (r.act1, r.act2):
            for core in range(2):
                buf[core, pl.ds(0, ROW), :] = jnp.zeros((ROW, HALF), BF16)
                buf[core, pl.ds(PX + ROW, ROW), :] = jnp.zeros((ROW, HALF), BF16)
        for buf in (r.gr1, r.gr2):
            for b in range(3):
                buf[b, pl.ds(0, ROW), :] = jnp.zeros((ROW, HALF), BF16)
                buf[b, pl.ds(PX + ROW, ROW), :] = jnp.zeros((ROW, HALF), BF16)
        r.wfp[...] = jnp.zeros((128, HALF), BF16)
        r.wfp[pl.ds(0, film_rows), :] = dot(r.wf[...], r.selp[: 2 * BLK, :HALF]).astype(BF16)
        if inside:
            ga.pass_z(1, 3, 2)
            gb.own()

        count = float(PX * 12)

        def fold(vals):
            return jnp.sum(vals.reshape(CHUNK // 8, 8, HALF), axis=0)

        def sums_of(fn, k):
            def step(i, carry):
                return tuple(a + fold(b) for a, b in zip(carry, fn(i)))

            zero = jnp.zeros((8, HALF), F32)
            return lax.fori_loop(0, 4, step, (zero,) * k)

        def group_mean(part):
            return jnp.sum(exact_dot(part, r.gmask[...]), axis=0, keepdims=True) / count

        def norm(load, which, total):
            mean = group_mean(total)
            (square,) = sums_of(lambda i: (jnp.square(load(i) - mean),), 1)
            inv = lax.rsqrt(group_mean(square) + EPS)
            r.stat[pl.ds(2 * which, 1), :] = mean
            r.stat[pl.ds(2 * which + 1, 1), :] = inv
            return mean, inv

        zero8 = jnp.zeros((8, HALF), F32)

        def norm_back(sums, load_grad, load_hat, coef, inv):
            plain, cross = sums
            means = exact_dot(jnp.concatenate([coef * plain, coef * cross], axis=0), r.gmask[...])
            plain_mean = jnp.sum(means[:8], axis=0, keepdims=True) / count
            cross_mean = jnp.sum(means[8:], axis=0, keepdims=True) / count
            outer, base, slope = inv * coef, inv * plain_mean, inv * cross_mean

            def chunk(i):
                return outer * load_grad(i) - base - load_hat(i) * slope

            return (
                jnp.sum(plain, axis=0, keepdims=True),
                jnp.sum(cross, axis=0, keepdims=True),
                chunk,
            )

        def transposed(name, core):
            ref = getattr(r, name).at[core]
            return rc(ref, ref, getattr(r, name + "_s").at[0], getattr(r, name + "_r").at[0], sib)

        def transpose_act(buf, base, name):
            out = getattr(r, name)
            for q in range(4):
                out[c, :, pl.ds(q * CHUNK, CHUNK)] = jnp.transpose(buf[c, pl.ds(base + q * CHUNK, CHUNK), :])
            transposed(name, c).start()

        def transposed_wait(name):
            copy = transposed(name, 1 - c)
            copy.wait_recv()
            copy.wait_send()

        head_wait(lambda p: r.mx_src.at[p], r.mx_dst, r.mx_s, r.mx_r)

        def unpack_mixed(i, carry):
            vals = unpack_pixels(r.mx_dst[i])
            r.mx[i] = vals
            return carry + fold(vals.astype(F32))

        mixed_sum = lax.fori_loop(0, 4, unpack_mixed, zero8)

        def mixed(i):
            return r.mx[i].astype(F32)

        if inside:
            ga.pass_v(1, 3)
        mean1, inv1 = norm(mixed, 0, mixed_sum)
        if inside:
            ga.pass_v(2)
        gain1, shift1 = prow(0), prow(3)
        act1 = Halves("act1", ROW)

        def affine(mean, inv, gain, shift):
            return inv * gain, shift - mean * (inv * gain)

        mul1, add1 = affine(mean1, inv1, gain1, shift1)

        def pre1(i):
            return mixed(i) * mul1 + add1

        act1.fill(lambda i: silu(pre1(i)).astype(BF16))
        dp_wait(lambda p: r.el.at[d], r.el, r.el_s, r.el_r)
        for j in range(n):
            r.em[pl.ds(2 * j, 2), :] = r.el[j]
        place = lax.broadcasted_iota(jnp.int32, (768, 128), 0) - film_rows * d
        lane = lax.broadcasted_iota(jnp.int32, (768, 128), 1)
        pick = jnp.where((place == lane) & (lane < film_rows), 1.0, 0.0).astype(BF16)
        r.esel[...] = dot(r.em[...].astype(BF16), pick)
        film_part = dot(r.esel[...].astype(BF16), r.wfp[...])
        for j in range(n):
            r.fp[j] = film_part[2 * j : 2 * j + 2]
        dp_start(lambda p: r.fp.at[p], r.fr, r.fr_s, r.fr_r)
        r.fr[d] = r.fp[d]
        if inside:
            swap.wait()
            got = r.sw_dst[...]
            keep0, keep2 = blocks[:, :128], blocks[:, 256:]
            r.p3[gc.at(0, 0, 0), 0] = pack_four(
                jnp.where(c == 0, keep0, got),
                jnp.where(c == 0, keep2, keep0),
                jnp.where(c == 0, got, keep2),
                r.wo[...],
            )
        act1.wait()
        transpose_act(r.act1, ROW, "act1_t")
        if inside:
            gb.pass_own()
            gb.pass_z(1, 3, 2)
            gc.own()
        def split_cot(m, carry):
            for core in range(2):
                r.cx_src[m * 2 + core] = pack_pixels(dot(r.cot[m], r.sel[core])).astype(BF16)
            return carry

        lax.fori_loop(0, 2, split_cot, 0)
        column = lax.broadcasted_iota(jnp.int32, (1, ROW, HALF), 1)
        not_first = jnp.where(column > 0, 1.0, 0.0)
        not_last = jnp.where(column < ROW - 1, 1.0, 0.0)

        def in_rows(vals, mask):
            return (vals.reshape(CHUNK // ROW, ROW, HALF) * mask).reshape(CHUNK, HALF)

        def from_left(vals):
            return in_rows(pltpu.roll(vals, 1, 0), not_first)

        def from_right(vals):
            return in_rows(pltpu.roll(vals, CHUNK - 1, 0), not_last)

        def conv(buf, g, store, between):
            weights = lambda: jnp.concatenate(
                [jnp.concatenate([wtap(g, 3 * a + b, ALL) for b in range(3)], axis=1) for a in range(3)], axis=0
            )

            total = zero8
            for i in range(2):
                left = jnp.concatenate([flat(buf, ROW * a, i, 2 * CHUNK) for a in range(3)], axis=1)
                out = dot(left, weights())
                for j in range(2):
                    part = out[j * CHUNK : j * CHUNK + CHUNK]
                    part = part[:, HALF : 2 * HALF] + from_left(part[:, :HALF]) + from_right(part[:, 2 * HALF :])
                    total = total + fold(store(2 * i + j, part))
                if i == 0:
                    between()
            return total

        if inside:
            k1.unpack(ga.blocks(0))
            ga.take(k1)

        dp_wait(lambda p: r.fp.at[p], r.fr, r.fr_s, r.fr_r)
        film_sum = r.fr[0]
        for j in range(1, n):
            film_sum = film_sum + r.fr[j]
        for m in range(2):
            for core in range(2):
                r.fx[m * 2 + core] = film_sum[m : m + 1, core * 128 : core * 128 + 128]
        head_start(lambda p: r.fx.at[p], r.fh, r.fh_s, r.fh_r)
        r.fh[h] = r.fx[h]

        def store_v2(i, vals):
            vals = vals + prow(6)
            r.v2[rows(i), :] = vals
            return vals

        v2_sum = conv(r.act1, k1, store_v2, (lambda: gb.pass_v(1, 3, 2)) if inside else lambda: None)
        head_wait(lambda p: r.fx.at[p], r.fh, r.fh_s, r.fh_r)
        scale = 1.0 + (jnp.concatenate([r.fh[0], r.fh[1]], axis=1) + prow(8))
        shift = jnp.concatenate([r.fh[2], r.fh[3]], axis=1) + prow(9)
        mean2, inv2 = norm(lambda i: r.v2[rows(i), :], 1, v2_sum)
        gain2, shift2 = prow(1), prow(4)
        act2 = Halves("act2", ROW)

        def hat2(i):
            return (r.v2[rows(i), :] - mean2) * inv2

        mul2, add2 = affine(mean2, inv2, gain2 * scale, shift2 * scale + shift)

        def pre2(i):
            return r.v2[rows(i), :] * mul2 + add2

        act2.fill(lambda i: silu(pre2(i)).astype(BF16))
        if inside:
            gc.pass_own()
            gc.pass_z(1, 3, 2)

        transpose_act(r.act2, ROW, "act2_t")
        act2.wait()
        if inside:
            k2.unpack(gb.blocks(0))
            gb.take(k2)

        head_start(lambda p: r.cx_src.at[p], r.cx_dst, r.cx_s, r.cx_r)
        r.cx_dst[h] = r.cx_src[h]

        def store_v3(i, vals):
            vals = mixed(i) + (vals + prow(7))
            r.v3[rows(i), :] = vals
            return vals

        v3_sum = conv(r.act2, k2, store_v3, (lambda: gc.pass_v(1, 3, 2)) if inside else lambda: None)
        mean3, inv3 = norm(lambda i: r.v3[rows(i), :], 2, v3_sum)
        gain3, shift3 = prow(2), prow(5)
        ai = Halves("ai", 0)

        def hat3(i):
            return (r.v3[rows(i), :] - mean3) * inv3

        mul3, add3 = affine(mean3, inv3, gain3, shift3)
        ai.fill(lambda i: (r.v3[rows(i), :] * mul3 + add3).astype(BF16))
        transpose_act(r.ai, 0, "ai_t")

        if inside:
            k3.unpack(gc.blocks(0))
            gc.take(k3)
        head_wait(lambda p: r.cx_src.at[p], r.cx_dst, r.cx_s, r.cx_r)

        def unpack_cot(i):
            r.cx[i] = unpack_pixels(r.cx_dst[i])

        loop(4, unpack_cot)
        dop = Parts("do")

        def cot_rows(i):
            return jnp.concatenate([r.cx[2 * i], r.cx[2 * i + 1]], axis=0)

        dop.fill(lambda i: dot_nt(cot_rows(i), wtap(k3, 3, half_of(1 - c))))

        ai.wait()
        bias_proj = [prow(10)[:, :128], prow(10)[:, 128:], None, None, prow(11)[:, :128], prow(11)[:, 128:]]

        def project(i):
            out = dot(flat(r.ai, 0, i, 2 * CHUNK), wproj(ALL))
            for k in range(6):
                part = out[:, k * 128 : k * 128 + 128]
                if bias_proj[k] is not None:
                    part = part + bias_proj[k]
                r.qkv[k, rows(i, 2 * CHUNK), :] = part.astype(BF16)

        each(2, project)

        def do_own(i):
            full = (dot_nt(cot_rows(i), wtap(k3, 3, half_of(c))) + dop.get(i)).astype(BF16)
            for k in range(2):
                r.dout[k, rows(i, 2 * CHUNK), :] = full[:, k * 128 : k * 128 + 128]

        each(2, do_own)

        factor = 1.0 / math.sqrt(HEAD_DIM)
        factor2 = factor * math.log2(math.e)
        att = []

        def transposes(k):
            r.kvt[k] = jnp.transpose(r.qkv[k + 2])

        loop(4, transposes)

        def att_copy(core, k):
            ref = r.att.at[core * 2 + k]
            return rc(ref, ref, r.att_s.at[k], r.att_r.at[k], sib)

        def att_t_copy(core, k):
            ref = r.att_t.at[core, pl.ds(pl.multiple_of(k * 128, 128), 128)]
            return rc(ref, ref, r.att_s.at[2 + k], r.att_r.at[2 + k], sib)

        def one_head(k):
            lows, grads = [], []
            for b in range(2):
                at = pl.ds(b * 2 * CHUNK, 2 * CHUNK)
                query = r.qkv[k, at, :]
                grad = r.dout[k, at, :]
                scores = dot_nt(r.qkv[2 + k], query)
                peak = jnp.max(scores, axis=0, keepdims=True)
                expo = jnp.exp2((scores - peak) * factor2)
                inverse = 1.0 / jnp.sum(expo, axis=0, keepdims=True)
                low = (expo * inverse).astype(BF16)
                got = dot(r.kvt[2 + k], low)
                got_low = got.astype(BF16)
                r.att_t[c, pl.ds(pl.multiple_of(k * 128, 128), 128), at] = got_low
                r.att[2 * c + k, at, :] = jnp.transpose(got_low)
                spread = jnp.sum(got * jnp.transpose(grad).astype(F32), axis=0, keepdims=True)
                probs_grad = dot_nt(r.qkv[4 + k], grad)
                scores_grad = ((probs_grad - spread) * inverse * expo).astype(BF16)
                back = dot(r.kvt[k], scores_grad)
                r.dproj[k, at, :] = (jnp.transpose(back) * factor).astype(BF16)
                lows.append(low)
                grads.append(scores_grad)
            att_copy(c, k).start()
            att_t_copy(c, k).start()
            r.dproj[4 + k] = dot(jnp.concatenate(lows, axis=1), r.dout[k]).astype(BF16)
            r.dproj[2 + k] = (dot(jnp.concatenate(grads, axis=1), r.qkv[k]) * factor).astype(BF16)

        loop(2, one_head)

        n3 = Parts("n3")

        def proj_rows(i):
            return jnp.concatenate([r.dproj[k, rows(i, 2 * CHUNK), :] for k in range(6)], axis=1)

        n3.fill(lambda i: dot_nt(proj_rows(i), wproj(half_of(1 - c))))

        def rows_of(act_t):
            return jnp.concatenate([act_t[p // 2, pl.ds(p % 2 * 128, BLK), :] for p in range(4)], axis=0)

        for k in range(2):
            copy = att_copy(1 - c, k)
            copy.wait_recv()
            copy.wait_send()

        def result(i):
            left = jnp.concatenate([r.att[p, rows(i), :] for p in range(4)], axis=1)
            branch = dot(left, wtap(k3, 3, ALL)) + prow(12)
            r.ro_src[i] = pack_pixels(r.v3[rows(i), :] + branch).astype(BF16)

        loop(4, result)
        head_start(lambda p: r.ro_src.at[p], r.ro_dst, r.ro_s, r.ro_r)
        r.ro_dst[h] = r.ro_src[h]

        if inside:
            red1, red2, red3 = Reduce("r1", 3), Reduce("r2", 3), Reduce("r3", 1)
            acc1, acc2, acc3 = r.r1_acc, r.r2_acc, r.r3_acc
        else:
            acc1, acc2, acc3 = r.first, r.second, r.attend

        transposed_wait("ai_t")
        for k in range(2):
            copy = att_t_copy(1 - c, k)
            copy.wait_recv()
            copy.wait_send()
        right = jnp.concatenate([r.dproj[k] for k in range(6)], axis=1)
        cot_all = jnp.concatenate([r.cx[i] for i in range(4)], axis=0)
        attend_out = dot(rows_of(r.ai_t), right)
        output_out = dot(rows_of(r.att_t), cot_all)
        for p, zc in enumerate(ALL):
            for yy in range(2):
                for xx in range(2):
                    row = p * BLK + yy * 48
                    tiles = [
                        attend_out[row : row + 48, (xx * 3 + j) * 128 : (xx * 3 + j) * 128 + 128] for j in range(3)
                    ]
                    acc3[0, slot(xx, yy), zc] = pack_four(
                        *tiles, output_out[row : row + 48, xx * 128 : xx * 128 + 128]
                    ).astype(acc3.dtype)
        if inside:
            red3.start(0)

        def proj_sums(i, carry):
            q = jnp.concatenate([r.dproj[0, rows(i), :], r.dproj[1, rows(i), :]], axis=1).astype(F32)
            val = jnp.concatenate([r.dproj[4, rows(i), :], r.dproj[5, rows(i), :]], axis=1).astype(F32)
            return (carry[0] + fold(q), carry[1] + fold(val), carry[2] + fold(r.cx[i].astype(F32)))

        qsum, vsum, csum = lax.fori_loop(0, 4, proj_sums, (zero8, zero8, zero8))
        r.sums[pl.ds(3 + 7, 1), :] = jnp.sum(qsum, axis=0, keepdims=True)
        r.sums[pl.ds(3 + 8, 1), :] = jnp.sum(vsum, axis=0, keepdims=True)
        r.sums[pl.ds(3 + 9, 1), :] = jnp.sum(csum, axis=0, keepdims=True)
        r.sums[pl.ds(13, 3), :] = jnp.zeros((3, HALF), F32)

        def n3_own(i, carry):
            both = dot_nt(proj_rows(i), wproj(half_of(c))) + n3.get(i)
            for j in range(2):
                vals = both[j * CHUNK : j * CHUNK + CHUNK]
                r.gtmp[rows(2 * i + j), :] = vals
                carry = carry[0] + fold(vals), carry[1] + fold(vals * hat3(2 * i + j))
            return carry

        sums3 = n3_own(1, n3_own(0, (zero8, zero8)))
        plain3, cross3, back3 = norm_back(sums3, lambda i: r.gtmp[rows(i), :], hat3, gain3, inv3)
        r.sums[pl.ds(2, 1), :] = cross3
        r.sums[pl.ds(3 + 2, 1), :] = plain3

        def shifted(buf, i, vals):
            buf[0, rows(i, CHUNK, ROW), :] = from_right(vals).astype(BF16)
            buf[1, rows(i, CHUNK, ROW), :] = vals.astype(BF16)
            buf[2, rows(i, CHUNK, ROW), :] = from_left(vals).astype(BF16)

        def residual_back(i, carry):
            vals = r.cx[i].astype(F32) + back3(i)
            r.gres[rows(i), :] = vals
            shifted(r.gr2, i, vals)
            return carry + fold(vals.astype(BF16).astype(F32))

        bias_two = lax.fori_loop(0, 4, residual_back, jnp.zeros((8, HALF), F32))
        r.sums[pl.ds(3 + 4, 1), :] = jnp.sum(bias_two, axis=0, keepdims=True)

        def act_back(buf, g, core, i, size):
            left = jnp.concatenate(
                [buf[b, rows(i, size, 2 * ROW - ROW * a), :] for a in range(3) for b in range(3)], axis=1
            )
            right = jnp.concatenate(
                [wtap(g, 3 * a + b, half_of(core)) for a in range(3) for b in range(3)], axis=1
            )
            return dot_nt(left, right)

        def conv_back(parts, buf, g):
            parts.fill(lambda i: act_back(buf, g, 1 - c, i, 2 * CHUNK))

        def conv_back_own(parts, buf, g, outer, hat):
            def own(i, carry):
                vals = act_back(buf, g, c, i, 2 * CHUNK) + parts.get(i)
                for j in range(2):
                    at = 2 * i + j
                    grad = vals[j * CHUNK : j * CHUNK + CHUNK] * outer(at)
                    r.gtmp[rows(at), :] = grad
                    carry = carry[0] + fold(grad), carry[1] + fold(grad * hat(at))
                return carry

            return own(1, own(0, (zero8, zero8)))

        def kernel_grad(act_t, buf, acc, after):
            def step(a):
                right = jnp.concatenate([buf[b, pl.ds(2 * ROW - ROW * a, PX), :] for b in range(3)], axis=1)
                out = dot(rows_of(act_t), right)
                for p, zc in enumerate(ALL):
                    for yy in range(2):
                        for xx in range(2):
                            row = p * BLK + yy * 48
                            tiles = [
                                out[row : row + 48, b * HALF + xx * 128 : b * HALF + xx * 128 + 128].astype(acc.dtype)
                                for b in range(3)
                            ]
                            acc[a, slot(xx, yy), zc] = pack_taps(*tiles)
                after(a)

            each(3, step)

        serve = inside
        d2 = Parts("d2")
        transposed_wait("act2_t")
        kernel_grad(r.act2_t, r.gr2, acc2, red2.start if inside else lambda a: None)
        if serve:
            red3.second(0, 1)
        conv_back(d2, r.gr2, k2)
        if serve:
            red2.second(0, 1)
        sums2 = conv_back_own(d2, r.gr2, k2, lambda i: silu_slope(pre2(i)), hat2)
        if serve:
            red2.second(1, 1)
            red3.third(0, 1)

        plain2, cross2, back2 = norm_back(sums2, lambda i: r.gtmp[rows(i), :], hat2, gain2 * scale, inv2)
        r.sums[pl.ds(1, 1), :] = scale * cross2
        r.sums[pl.ds(3 + 1, 1), :] = scale * plain2
        film_scale_term = gain2 * cross2 + shift2 * plain2
        r.sums[pl.ds(3 + 5, 1), :] = film_scale_term
        r.sums[pl.ds(3 + 6, 1), :] = plain2
        for j in range(2):
            r.ft[j] = film_scale_term[:, j * 128 : j * 128 + 128]
            r.ft[2 + j] = plain2[:, j * 128 : j * 128 + 128]
        head_start(lambda p: r.ft.at[p], r.th, r.th_s, r.th_r)
        r.th[h] = r.ft[h]

        def first_back(i, carry):
            vals = back2(i)
            shifted(r.gr1, i, vals)
            return carry + fold(vals.astype(BF16).astype(F32))

        bias_one = lax.fori_loop(0, 4, first_back, jnp.zeros((8, HALF), F32))
        r.sums[pl.ds(3 + 3, 1), :] = jnp.sum(bias_one, axis=0, keepdims=True)

        if serve:
            red2.second(2, 1)
            red2.third(0, 1)
            red2.third(1, 1)

        head_wait(lambda p: r.ft.at[p], r.th, r.th_s, r.th_r)
        for m in range(2):
            r.fa[d, pl.ds(m, 1), :] = jnp.concatenate([r.th[2 * m], r.th[2 * m + 1]], axis=1)
        dp_start(lambda p: r.fa.at[d], r.fa, r.fa_s, r.fa_r)

        d1 = Parts("d1")

        def after_chunk(a):
            if serve:
                red1.start(a)
                if a == 1:
                    red2.third(2, 1)

        transposed_wait("act1_t")
        kernel_grad(r.act1_t, r.gr1, acc1, after_chunk)
        conv_back(d1, r.gr1, k1)
        if serve:
            red1.second(0, 1)

        dp_wait(lambda p: r.fa.at[d], r.fa, r.fa_s, r.fa_r)
        for j in range(n):
            r.fta[pl.ds(2 * j, 2), :] = r.fa[j]
        film_block = dot_tn_high(r.esel[...], r.fta[...])
        r.film[...] = jnp.concatenate([film_block[:film_rows, :BLK], film_block[:film_rows, 128 : 128 + BLK]], axis=1)
        embed_part = dot_nt_high(r.fta[...], r.wfp[...].astype(F32))
        for j in range(n):
            r.ep[j] = embed_part[2 * j : 2 * j + 2]
        dp_start(lambda p: r.ep.at[p], r.er, r.er_s, r.er_r)
        r.er[d] = r.ep[d]

        def hat1(i):
            return (mixed(i) - mean1) * inv1

        sums1 = conv_back_own(d1, r.gr1, k1, lambda i: silu_slope(pre1(i)), hat1)
        if serve:
            red1.second(1, 1)

        plain1, cross1, back1 = norm_back(sums1, lambda i: r.gtmp[rows(i), :], hat1, gain1, inv1)
        r.sums[pl.ds(0, 1), :] = cross1
        r.sums[pl.ds(3, 1), :] = plain1
        r.ad[d] = r.sums[...]
        dp_start(lambda p: r.ad.at[d], r.ad, r.ad_s, r.ad_r)

        if serve:
            red1.second(2, 1)
            red1.third(0, 1)
        keep, _ = plan(r.steps[x], HALF)

        def image_back(i):
            return pack_pixels(keep * (r.gres[rows(i), :] + back1(i))).astype(BF16)

        for k in (2, 1, 3):
            peer = lax.rem(h + k, 4)
            r.io_src[peer] = image_back(peer)
            rc(r.io_src.at[peer], r.io_dst.at[h], r.io_s.at[k], r.io_r.at[h], (d, peer)).start()
        r.io_dst[h] = image_back(h)
        if serve:
            red1.third(1, 1)
            red1.third(2, 1)

        dp_wait(lambda p: r.ep.at[p], r.er, r.er_s, r.er_r)
        r.eh[h] = r.er[...]
        head_start(lambda p: r.eh.at[h], r.eh, r.eh_s, r.eh_r)
        dp_wait(lambda p: r.ad.at[d], r.ad, r.ad_s, r.ad_r)
        total = r.ad[0]
        for j in range(1, n):
            total = total + r.ad[j]
        r.hb[h] = total
        head_start(lambda p: r.hb.at[h], r.hb, r.hb_s, r.hb_r)
        head_wait(lambda p: r.ro_src.at[p], r.ro_dst, r.ro_s, r.ro_r)

        if inside:
            red2.finish(((0, 1), (1, 1), (2, 1)))
            for a in range(3):
                r.second[a] = red2.last(a)

        head_wait(lambda p: r.hb.at[h], r.hb, r.hb_s, r.hb_r)
        even = r.hb[0] + r.hb[2]
        odd = r.hb[1] + r.hb[3]
        wide = jnp.concatenate(
            [even[:, :BLK], odd[:, :BLK], even[:, 128 : 128 + BLK], odd[:, 128 : 128 + BLK]], axis=1
        )
        r.gains_out[...] = wide[0:3]
        r.biases_out[...] = wide[3:13]

        head_wait(lambda p: r.eh.at[h], r.eh, r.eh_s, r.eh_r)
        pieces = []
        for j in range(n):
            piece = (r.eh[0, j] + r.eh[1, j]) + (r.eh[2, j] + r.eh[3, j])
            pieces.append(piece[:, :film_rows])
        r.embed_grad[...] = jnp.concatenate(pieces, axis=1) * silu_slope(r.emb[...].astype(F32))

        head_wait(lambda p: r.io_src.at[p], r.io_dst, r.io_s, r.io_r)

        if inside:
            red3.finish(((0, 1),))
            tiles = unpack_four(red3.last(0))
            r.sb_src[...] = jnp.where(c == 0, tiles[2], tiles[0])
            back = rc(r.sb_src, r.sb_dst, r.sb_s.at[0], r.sb_r.at[0], sib)
            back.start()
            r.output[...] = tiles[3]
            for part in (ga, gb, gc):
                part.finish()
            red1.finish(((0, 1), (1, 1), (2, 1)))
            for a in range(3):
                r.first[a] = red1.last(a)
            back.wait()
            r.attend[:, 0:128] = jnp.where(c == 0, tiles[0], tiles[1])
            r.attend[:, 128:256] = r.sb_dst[...]
            r.attend[:, 256:384] = jnp.where(c == 0, tiles[1], tiles[2])

    return kernel


def make_writer(names_in, names_out):
    def kernel(*refs):
        count, wide = len(names_in), len(names_out)
        far_in, far_out = refs[:count], refs[count : count + wide]
        near_in, near_out = refs[count + wide : 2 * count + wide], refs[2 * count + wide : 2 * count + 2 * wide]
        sem_in, sem_out = refs[-2:]
        src, dst = Names(names_in, near_in), Names(names_out, near_out)
        loads = {
            name: pltpu.make_async_copy(far_in[i], near_in[i], sem_in.at[i]) for i, name in enumerate(names_in)
        }
        stores = {
            name: pltpu.make_async_copy(near_out[i], far_out[i], sem_out.at[i]) for i, name in enumerate(names_out)
        }
        for name in ("sel", "ro_dst", "io_dst"):
            loads[name].start()
        for name in names_in:
            if name not in ("sel", "ro_dst", "io_dst"):
                loads[name].start()
        loads["sel"].wait()
        for name, packed in (("result", "ro_dst"), ("image_grad", "io_dst")):
            loads[packed].wait()
            ref = getattr(src, packed)
            for m in range(2):
                getattr(dst, name)[m] = dot_nt(unpack_pixels(ref[2 * m]), src.sel[0]) + dot_nt(
                    unpack_pixels(ref[2 * m + 1]), src.sel[1]
                )
            stores[name].start()
        for name in ("first", "second"):
            if name in names_out:
                loads[name].wait()
                for a in range(3):
                    block = getattr(src, name)[a]
                    getattr(dst, name)[3 * a] = block[:48, :BLK]
                    getattr(dst, name)[3 * a + 1] = block[48:96, :BLK]
                    getattr(dst, name)[3 * a + 2] = last_tap(block)[:, :BLK]
                stores[name].start()
        if "attend" in names_out:
            loads["attend"].wait()
            dst.attend[...] = jnp.concatenate([src.attend[:, j * 128 : j * 128 + BLK] for j in range(3)], axis=1)
            stores["attend"].start()
            loads["output"].wait()
            dst.output[...] = src.output[:, :BLK]
            stores["output"].start()
        for name in ("embed_grad", "film", "gains_out", "biases_out"):
            loads[name].wait()
            getattr(dst, name)[...] = getattr(src, name)[...]
            stores[name].start()
        for name in names_out:
            stores[name].wait()

    return kernel


def per_device(n, *args):
    (
        images,
        noise_field,
        time_steps,
        embedding,
        first_kernel,
        second_kernel,
        film_weight,
        attend_weight,
        output_weight,
        norm_gains,
        biases,
        cotangent,
    ) = args
    inside = n == 8
    maps, height, width, channels = images.shape
    flat_shape = (maps, height * width, channels)
    film_rows = film_weight.shape[0]
    inputs = dict(
        steps=time_steps,
        images=images.reshape(flat_shape),
        noise=noise_field.reshape(flat_shape),
        cot=cotangent.reshape(flat_shape),
        emb=embedding,
        k1=first_kernel.reshape((9,) + first_kernel.shape[2:]),
        k2=second_kernel.reshape((9,) + second_kernel.shape[2:]),
        wf=film_weight,
        wa=attend_weight,
        wo=output_weight,
        gains=norm_gains,
        biases=biases,
        sel=jnp.asarray(channel_lanes(), BF16),
        gmask=jnp.asarray(group_mask(), BF16),
        selp=jnp.asarray(block_lanes(3), BF16),
    )
    shapes = dict(
        ro_dst=(4, 384, 128),
        io_dst=(4, 384, 128),
        embed_grad=embedding.shape,
        first=(3, 112, 128),
        second=(3, 112, 128),
        film=film_weight.shape,
        attend=(48, 384),
        output=(48, 128),
        gains_out=norm_gains.shape,
        biases_out=biases.shape,
    )
    names_in, names_out = list(INPUTS), list(OUTPUTS)
    core = lax.axis_index("head") % 2
    if not inside:
        def whole(array, row_axis):
            array = lax.all_gather(array, "dp", axis=row_axis, tiled=True)
            return lax.all_gather(array, "head", axis=array.ndim - 1, tiled=True)

        def spread(array, count):
            taps = array.shape[0]
            array = array.reshape(taps, 4, 2, 48, 2, 2, BLK)
            array = lax.dynamic_index_in_dim(array, core, 5, keepdims=False)
            array = jnp.transpose(array, (2, 4, 1, 0, 3, 5))
            array = jnp.pad(array, ((0, 0),) * 5 + ((0, 32),))
            return array.reshape(4, 4, taps * 48, 128)

        full_a = whole(attend_weight, 0).reshape(384, 2, 3, 2, BLK)
        full_a = jnp.transpose(full_a, (2, 0, 1, 3, 4)).reshape(3, 384, 384)
        full_o = whole(output_weight, 0)[None]
        for name, last, array in (("g1", "t1", first_kernel), ("g2", "t2", second_kernel)):
            blocks = spread(whole(array, 2).reshape(9, 384, 384), 9).reshape(4, 4, 3, 3, 48, 128)
            two = blocks[:, :, :, :2].reshape(4, 4, 3, 96, 128)
            inputs[name] = jnp.pad(two, ((0, 0),) * 3 + ((0, 16), (0, 0))).reshape(4, 4, 336, 128)
            inputs[last] = blocks[:, :, :, 2].reshape(4, 4, 144, 128)
        inputs["g3"] = spread(jnp.concatenate([full_a, full_o], axis=0), 4)
        names_in += ["g1", "g2", "t1", "t2", "g3"]
        shapes["first"] = shapes["second"] = (3, 4, 4, 112, 128)
        shapes["attend"] = (1, 4, 4, 144, 128)
        del shapes["output"]
        names_out.remove("output")
    items = scratch_list(n, inside, inputs)
    smem = pl.BlockSpec(memory_space=pltpu.SMEM)
    vmem = pl.BlockSpec(memory_space=pltpu.VMEM)
    outs = pl.pallas_call(
        make_kernel(
            n,
            inside,
            [name + "_far" if name in FAR else name for name in names_in] + names_out + [name for name, _ in items],
        ),
        out_shape=[
            jax.ShapeDtypeStruct(shapes[name], BF16 if name in ("ro_dst", "io_dst") else F32) for name in names_out
        ],
        in_specs=[
            smem if name == "steps" else pl.BlockSpec(memory_space=pl.ANY) if name in FAR else vmem
            for name in names_in
        ],
        out_specs=[vmem] * len(names_out),
        scratch_shapes=[item for _, item in items],
        compiler_params=pltpu.CompilerParams(
            collective_id=0, has_side_effects=True, vmem_limit_bytes=63 * 1024 * 1024
        ),
        name="blocks",
    )(*[inputs[name] for name in names_in])
    raw = dict(zip(names_out, outs))
    final = dict(
        result=flat_shape,
        image_grad=flat_shape,
        embed_grad=embedding.shape,
        film=film_weight.shape,
        gains_out=norm_gains.shape,
        biases_out=biases.shape,
    )
    if inside:
        final.update(first=(9, 48, BLK), second=(9, 48, BLK), attend=attend_weight.shape, output=output_weight.shape)
    names_last = [name for name in names_out if inside or name not in ("first", "second", "attend")] + ["sel"]
    names_final = list(final)
    given = [inputs["sel"] if name == "sel" else raw[name] for name in names_last]
    far = pl.BlockSpec(memory_space=pl.ANY)
    outs = pl.pallas_call(
        make_writer(names_last, names_final),
        out_shape=[jax.ShapeDtypeStruct(final[name], F32) for name in names_final],
        in_specs=[far] * len(names_last),
        out_specs=[far] * len(names_final),
        scratch_shapes=[pltpu.VMEM(array.shape, array.dtype) for array in given]
        + [pltpu.VMEM(final[name], F32) for name in names_final]
        + [pltpu.SemaphoreType.DMA((len(names_last),)), pltpu.SemaphoreType.DMA((len(names_final),))],
        compiler_params=pltpu.CompilerParams(vmem_limit_bytes=63 * 1024 * 1024),
        name="outputs",
    )(*given)
    out = dict(zip(names_final, outs))
    if not inside:

        def blocks_of(array, size):
            parts = [array[..., k * 48 : k * 48 + 48, :BLK] for k in range(size)]
            if size == 2:
                lanes = [array[..., k * 32 : k * 32 + 32, BLK:] for k in range(3)]
                lanes = jnp.concatenate(lanes, axis=-1)
                parts.append(jnp.concatenate([lanes, array[..., 96:112, :BLK]], axis=-2))
            else:
                lanes = [array[..., k * 48 : k * 48 + 48, BLK:] for k in range(3)]
                parts.append(jnp.concatenate(lanes, axis=-1))
            array = jnp.stack(parts, axis=1)
            array = array.reshape(array.shape[:2] + (2, 2, 4, 48, BLK))
            taps = array.shape[0] * array.shape[1]
            array = jnp.transpose(array, (0, 1, 4, 2, 5, 3, 6)).reshape(taps, 384, 2, 1, BLK)
            both = jnp.concatenate([array, jnp.zeros_like(array)], axis=3)
            return jnp.where(core == 0, both, both[:, :, :, ::-1]).reshape(taps, 384, 384)

        def shared(array, axis):
            array = lax.psum_scatter(array, "head", scatter_dimension=array.ndim - 1, tiled=True)
            return lax.psum_scatter(array, "dp", scatter_dimension=axis, tiled=True)

        out["first"] = shared(blocks_of(raw["first"], 2), 1)
        out["second"] = shared(blocks_of(raw["second"], 2), 1)
        both = blocks_of(raw["attend"], 3)
        joined = both[:3].reshape(3, 384, 2, 2, BLK)
        joined = jnp.transpose(joined, (1, 2, 0, 3, 4)).reshape(384, 1152)
        out["attend"] = shared(joined, 0)
        out["output"] = shared(both[3], 0)
    return (
        out["result"].reshape(images.shape),
        out["image_grad"].reshape(images.shape),
        out["embed_grad"],
        out["first"].reshape(first_kernel.shape),
        out["second"].reshape(second_kernel.shape),
        out["film"],
        out["attend"],
        out["output"],
        out["gains_out"],
        out["biases_out"],
    )


def solution(mesh):
    n = mesh.shape["dp"]
    field = P("dp", "head", None, None)
    taps = P(None, None, "dp", "head")
    both = P("dp", "head")
    return jax.shard_map(
        lambda *args: per_device(n, *args),
        mesh=mesh,
        in_specs=(field, field, P("dp"), P("dp", None), taps, taps, both, both, both, P(), P(), field),
        out_specs=(field, field, P("dp", None), taps, taps, both, both, both, P(), P()),
        check_vma=False,
    )
```

profile of v0, /device:TPU:0, one launch (start us, length us, event | category | flops | bytes accessed | tf_op | source)
XLA Modules:
  0.0 111.3 jit_solution(16498063066585271509)
XLA Ops:
  0.6 107.1 %blocks.1 = (bf16[4,384,128]{2,1,0:T(8,128)(2,1)}, bf16[4,384,128]{2,1,0:T(8,128)(2,1)}, f32[2,768]{1,0:T(2,128)}, f32[3,112,128]{2,1,0:T(8,128)}, f32[3,112,128...) custom-call(s32[2]{0:T(128)} %refs_0_.1, ...), custom_call_target="tpu_custom_call" | custom-call | tf_op jit(solution)/shard_map/blocks/pallas_call | solution.py:1415
  107.8 3.3 %outputs.1 = (f32[2,256,384]{2,1,0:T(8,128)}, f32[2,256,384]{2,1,0:T(8,128)}, f32[2,768]{1,0:T(2,128)}, f32[96,192]{1,0:T(8,128)}, f32[3,384]{1,0:T(4,128)}, /*i...) custom-call(bf16[4,384,128]{2,1,0:T(8,128)(2,1)} %get-tuple-element.3, ...), custom_call_target="tpu_custom_call" | custom-call | tf_op jit(solution)/shard_map/outputs/pallas_call | solution.py:1450
where the time goes:
time: 111 us
  Pallas kernels  110 us (99%)
    pallas_call x1, Pallas kernels, per_device(): pl.pallas_call(make_kernel(n, inside, [name + '_far' if name in FAR else...  107 us
    pallas_call x1, Pallas kernels, per_device(): pl.pallas_call(make_writer(names_last, names_final), out_shape=[jax.Shape...  3.35 us

commit v1 on v0

--- a/solution.py
+++ b/solution.py
@@ -449,9 +449,11 @@
                 dev = (d + (1 - o) * (1 - 2 * y), h + o * (2 - 4 * x))
                 return rc(ref, ref, self.ws.at[2 * i + far_v], self.wr.at[2 * i + far_v], dev)
 
-            def own(self):
+            def own_z(self):
                 for k in range(1, 4):
                     self.zcopy(k).start()
+
+            def own(self):
                 self.vcopy(0, 0).start()
                 self.wcopy(0, 0, 0).start()
 
@@ -646,6 +648,7 @@
                 r.g1[ga.at(0, 0, 0), 0, pl.ds(a * 112, 112), :] = pack_taps(*[r.k1[3 * a + b] for b in range(3)])
         pl.semaphore_wait(barrier, n - 1 + 3)
         if inside:
+            ga.own_z()
             ga.own()
 
         for name in FAR:
@@ -696,7 +699,7 @@
         r.wfp[pl.ds(0, film_rows), :] = dot(r.wf[...], r.selp[: 2 * BLK, :HALF]).astype(BF16)
         if inside:
             ga.pass_z(1, 3, 2)
-            gb.own()
+            gb.own_z()
 
         count = float(PX * 12)
 
@@ -771,6 +774,7 @@
         mean1, inv1 = norm(mixed, 0, mixed_sum)
         if inside:
             ga.pass_v(2)
+            gb.own()
         gain1, shift1 = prow(0), prow(3)
         act1 = Halves("act1", ROW)
 
@@ -810,7 +814,7 @@
         if inside:
             gb.pass_own()
             gb.pass_z(1, 3, 2)
-            gc.own()
+            gc.own_z()
         def split_cot(m, carry):
             for core in range(2):
                 r.cx_src[m * 2 + core] = pack_pixels(dot(r.cot[m], r.sel[core])).astype(BF16)
@@ -866,7 +870,7 @@
             r.v2[rows(i), :] = vals
             return vals
 
-        v2_sum = conv(r.act1, k1, store_v2, (lambda: gb.pass_v(1, 3, 2)) if inside else lambda: None)
+        v2_sum = conv(r.act1, k1, store_v2, (lambda: (gb.pass_v(1, 3, 2), gc.own())) if inside else lambda: None)
         head_wait(lambda p: r.fx.at[p], r.fh, r.fh_s, r.fh_r)
         scale = 1.0 + (jnp.concatenate([r.fh[0], r.fh[1]], axis=1) + prow(8))
         shift = jnp.concatenate([r.fh[2], r.fh[3]], axis=1) + prow(9)

time: 111 us -> 114 us (1.027)
  Pallas kernels: 110 us -> 113 us
    pallas_call x1, Pallas kernels: 107 us -> 109 us  [per_device(): pl.pallas_call(make_kernel(n, inside, [name + '_far' if name in FAR else...]
where the time goes in v1:
time: 114 us
  Pallas kernels  113 us (99%)
    pallas_call x1, Pallas kernels, per_device(): pl.pallas_call(make_kernel(n, inside, [name + '_far' if name in FAR else...  109 us
    pallas_call x1, Pallas kernels, per_device(): pl.pallas_call(make_writer(names_last, names_final), out_shape=[jax.Shape...  3.34 us

profile of v1, /device:TPU:0, one launch (start us, length us, event | category | flops | bytes accessed | tf_op | source)
XLA Modules:
  0.0 113.7 jit_solution(17694623051592331360)
XLA Ops:
  0.6 109.5 %blocks.1 = (bf16[4,384,128]{2,1,0:T(8,128)(2,1)}, bf16[4,384,128]{2,1,0:T(8,128)(2,1)}, f32[2,768]{1,0:T(2,128)}, f32[3,112,128]{2,1,0:T(8,128)}, f32[3,112,128...) custom-call(s32[2]{0:T(128)} %refs_0_.1, ...), custom_call_target="tpu_custom_call" | custom-call | tf_op jit(solution)/shard_map/blocks/pallas_call | solution.py:1419
  110.1 3.3 %outputs.1 = (f32[2,256,384]{2,1,0:T(8,128)}, f32[2,256,384]{2,1,0:T(8,128)}, f32[2,768]{1,0:T(2,128)}, f32[96,192]{1,0:T(8,128)}, f32[3,384]{1,0:T(4,128)}, /*i...) custom-call(bf16[4,384,128]{2,1,0:T(8,128)(2,1)} %get-tuple-element.3, ...), custom_call_target="tpu_custom_call" | custom-call | tf_op jit(solution)/shard_map/outputs/pallas_call | solution.py:1454
